TPU v7x, 128 devices: a whole 4x4x4 slice. The times are simulated.
128 devices in a mesh: fsdp: 16 (over z, y_lo, core), tp: 8 (over y_hi, x).
Axes of the slice: x: 4, y: 4 (y_hi: 2, y_lo: 2; y = y_hi * 2 + y_lo), z: 4, core: 2. Of those that a mesh axis runs over, the one named last changes fastest.
Arguments:
- block_input: bfloat16 [16384, 2048], P(('fsdp', 'tp')), may hold values from -6 to 6
- norm_gain: bfloat16 [2048], P('fsdp'), may hold values from 0.099609375 to 1.8984375
- norm_bias: bfloat16 [2048], P('fsdp'), may hold values from -3 to 3
- qkv_weight: bfloat16 [2048, 3, 2048], P('fsdp', None, 'tp'), may hold values from -0.125 to 0.125
- qkv_bias: bfloat16 [3, 2048], P(None, 'tp'), may hold values from -3 to 3
- dense_weight: bfloat16 [2048, 2048], P('tp', 'fsdp'), may hold values from -1 to 1
- dense_bias: bfloat16 [2048], P('fsdp'), may hold values from -3 to 3
- up_weight: bfloat16 [2048, 8192], P('fsdp', 'tp'), may hold values from -0.125 to 0.125
- up_bias: bfloat16 [8192], P('tp'), may hold values from -3 to 3
- down_weight: bfloat16 [8192, 2048], P('tp', 'fsdp'), may hold values from -0.0625 to 0.0625
- down_bias: bfloat16 [2048], P('fsdp'), may hold values from -3 to 3
- cotangent: bfloat16 [16384, 2048], P(('fsdp', 'tp')), may hold values from -6 to 6
Outputs:
- block_output: bfloat16 [16384, 2048], P(('fsdp', 'tp'))
- input_grad: bfloat16 [16384, 2048], P(('fsdp', 'tp'))
- grad_norm_gain: float32 [2048], P('fsdp')
- grad_norm_bias: float32 [2048], P('fsdp')
- grad_qkv_weight: float32 [2048, 3, 2048], P('fsdp', None, 'tp')
- grad_qkv_bias: float32 [3, 2048], P(None, 'tp')
- grad_dense_weight: float32 [2048, 2048], P('tp', 'fsdp')
- grad_dense_bias: float32 [2048], P('fsdp')
- grad_up_weight: float32 [2048, 8192], P('fsdp', 'tp')
- grad_up_bias: float32 [8192], P('tp')
- grad_down_weight: float32 [8192, 2048], P('tp', 'fsdp')
- grad_down_bias: float32 [2048], P('fsdp')
All inputs are finite; a program needn't handle non-finite values.
Results may differ from a plain program's by a relative error of at most 0.02.
Values may be sent and summed in bfloat16 or wider, within the bound.
A program may use at most 128 MiB of HBM per device.

v0:
```python
import jax
import jax.numpy as jnp
import numpy as np
from jax import lax
from jax.experimental import pallas as pl
from jax.experimental.pallas import tpu as pltpu
from jax.sharding import PartitionSpec as P

HD = 64
ROT = 32
SEQ_LEN = 1024
EPS = 1e-05
D = 2048
TOK = 128
WA = 1792
WB = 1280
GELU = 0.7978845608028654
F32 = jnp.float32
BF16 = jnp.bfloat16
MESH = pl.DeviceIdType.MESH
ANY = pl.BlockSpec(memory_space=pl.ANY)
VMEM = pl.BlockSpec(memory_space=pltpu.VMEM)


def place():
    f = lax.axis_index("fsdp")
    t = lax.axis_index("tp")
    return f, t, lax.div(f, 4), lax.rem(lax.div(f, 2), 2), lax.rem(f, 2), lax.div(t, 4), lax.rem(t, 4)


def greet(peers):
    barrier = pltpu.get_barrier_semaphore()
    for peer in peers:
        pl.semaphore_signal(barrier, inc=1, device_id=peer, device_id_type=MESH)
    pl.semaphore_wait(barrier, len(peers))


def all_peers(f, t):
    peers = [(lax.rem(f + d, 16), t) for d in range(1, 16)]
    return peers + [(f, lax.rem(t + d, 8)) for d in range(1, 8)]


def remote(src, dst, ssem, rsem, to):
    return pltpu.make_async_remote_copy(
        src_ref=src, dst_ref=dst, send_sem=ssem, recv_sem=rsem, device_id=to, device_id_type=MESH
    )


class Group:
    def __init__(self, axis):
        f, t, z, yl, c, yh, x = place()
        self.axis = axis
        if axis == "tp":
            self.k, self.r, self.c = x, yh, 0
            self.dev = lambda r, k: (f, r * 4 + k)
        else:
            self.k, self.r, self.c = z, yl, c
            self.dev = lambda r, k: ((k * 2 + r) * 2 + c, t)
            self.sib = ((z * 2 + yl) * 2 + 1 - c, t)
        self.up, self.down, self.far = lax.rem(self.k + 1, 4), lax.rem(self.k + 3, 4), lax.rem(self.k + 2, 4)
        self.other = 1 - self.r

    def index(self, r, k, c=None):
        if self.axis == "tp":
            return r * 4 + k
        return (k * 2 + r) * 2 + (self.c if c is None else c)


class Mover:
    def __init__(self, group, ssem, rsem):
        self.g, self.ssem, self.rsem, self.plan, self.lands = group, ssem, rsem, {}, {}

    def send(self, *numbers):
        for n in numbers:
            src, dst, to = self.plan[n]
            remote(src, dst, self.ssem.at[n], self.rsem.at[n], to).start()

    def recv(self, *numbers):
        for n in numbers:
            land = self.lands[n]
            remote(land, land, self.ssem.at[n], self.rsem.at[n], self.plan[n][2]).wait_recv()

    def sent(self):
        for n, (src, dst, to) in self.plan.items():
            remote(src, dst, self.ssem.at[n], self.rsem.at[n], to).wait_send()


class Gather(Mover):
    def __init__(self, group, block, half, ssem, rsem, sibling=False):
        super().__init__(group, ssem, rsem)
        g = group
        self.sibling = sibling

        def add(n, src, land, to):
            self.plan[n], self.lands[n] = (src, src, to), land

        add(0, block(g.index(g.r, g.k)), block(g.index(g.other, g.k)), g.dev(g.other, g.k))
        for row, r in enumerate((g.r, g.other)):
            up, down = g.dev(g.r, g.up), g.dev(g.r, g.down)
            here = g.index(r, g.k)
            above, below, far = g.index(r, g.up), g.index(r, g.down), g.index(r, g.far)
            n = 1 + 4 * row
            add(n, half(here, 0), half(below, 0), up)
            add(n + 1, half(here, 1), half(above, 1), down)
            add(n + 2, half(here, 1), half(below, 1), up)
            add(n + 3, half(here, 0), half(above, 0), down)
            add(9 + 2 * row, half(below, 0), half(far, 0), up)
            add(10 + 2 * row, half(above, 1), half(far, 1), down)
        if sibling:
            for row, r in enumerate((g.r, g.other)):
                for j, k in enumerate((g.k, g.down, g.up, g.far)):
                    add(13 + 4 * row + j, block(g.index(r, k)), block(g.index(r, k, 1 - g.c)), g.sib)

    def pass_on(self, *numbers):
        if self.sibling:
            self.send(*numbers)

    def ring(self, row):
        n = 1 + 4 * row
        self.send(n, n + 1, n + 2, n + 3)
        self.pass_on(13 + 4 * row)

    def pair_send(self):
        self.send(0)

    def pair_recv(self):
        self.recv(0)
        self.ring(1)

    def forward(self, row):
        n = 1 + 4 * row
        self.recv(n)
        self.send(9 + 2 * row)
        self.recv(n + 1)
        self.send(10 + 2 * row)

    def near(self, row):
        n = 1 + 4 * row
        self.recv(n + 2, n + 3)
        self.pass_on(14 + 4 * row, 15 + 4 * row)

    def far(self, row):
        self.recv(9 + 2 * row, 10 + 2 * row)
        self.pass_on(16 + 4 * row)

    def finish(self):
        if self.sibling:
            self.recv(*range(13, 21))
        self.sent()


def add_rows(out, ins, chunk):
    @pl.loop(0, out.shape[0] // chunk)
    def _(i):
        rows = pl.ds(pl.multiple_of(i * chunk, chunk), chunk)
        total = ins[0][rows, :].astype(F32)
        for ref in ins[1:]:
            total = total + ref[rows, :].astype(F32)
        out[rows, :] = total.astype(out.dtype)


class Scatter(Mover):
    def __init__(self, group, block, half, far, near, pair, ssem, rsem, chunk, sib=None):
        super().__init__(group, ssem, rsem)
        g = group
        self.block, self.half, self.chunk = block, half, chunk
        self.far_ref, self.near_ref, self.pair_ref, self.sib_ref = far, near, pair, sib
        self.rows = (g.other, g.r)
        self.order = [(g.other, g.far), (g.r, g.far), (g.other, g.up), (g.other, g.down)]
        self.order += [(g.r, g.up), (g.r, g.down), (g.other, g.k), (g.r, g.k)]
        size = near.shape[2] // 2

        def add(n, src, dst, to):
            self.plan[n], self.lands[n] = (src, dst, to), dst

        for row, r in enumerate(self.rows):
            n = 6 * row
            up, down = g.dev(g.r, g.up), g.dev(g.r, g.down)
            above, below, far_at = g.index(r, g.up), g.index(r, g.down), g.index(r, g.far)
            add(n, half(far_at, 0), far.at[row, 0], up)
            add(n + 1, half(far_at, 1), far.at[row, 1], down)
            add(n + 2, half(above, 1), near.at[row, 0, pl.ds(size, size)], up)
            add(n + 3, half(below, 0), near.at[row, 1, pl.ds(0, size)], down)
            add(n + 4, half(above, 0), near.at[row, 0, pl.ds(0, size)], up)
            add(n + 5, half(below, 1), near.at[row, 1, pl.ds(size, size)], down)
        add(12, block(g.index(g.other, g.k)), pair, g.dev(g.other, g.k))
        if sib is not None:
            for s, (r, k) in enumerate(self.order):
                add(13 + s, block(g.index(r, k, 1 - g.c)), sib.at[s], g.sib)

    def chip(self, s):
        r, k = self.order[s]
        return k * 2 + r

    def sib_send(self, s):
        self.send(13 + s)

    def sib_add(self, s):
        self.recv(13 + s)
        mine = self.block(self.g.index(*self.order[s]))
        add_rows(mine, [mine, self.sib_ref.at[s]], self.chunk)

    def far(self, row):
        self.send(6 * row, 6 * row + 1)

    def free(self, row):
        self.send(6 * row + 2, 6 * row + 3)

    def relay(self, row):
        for way, k in ((0, self.g.up), (1, self.g.down)):
            n = 6 * row + way
            self.recv(n)
            mine = self.half(self.g.index(self.rows[row], k), way)
            add_rows(mine, [mine, self.far_ref.at[row, way]], self.chunk)
            self.send(n + 4)

    def pair(self):
        self.recv(2, 3, 4, 5)
        mine = self.block(self.g.index(*self.order[6]))
        add_rows(mine, [mine, self.near_ref.at[0, 0], self.near_ref.at[0, 1]], self.chunk)
        self.send(12)

    def last(self):
        self.recv(8, 9, 10, 11, 12)
        return [self.block(self.g.index(*self.order[7])), self.near_ref.at[1, 0], self.near_ref.at[1, 1], self.pair_ref]


def dot_nn(a, b):
    return jnp.dot(a, b, preferred_element_type=F32)


def dot_nt(a, b):
    return lax.dot_general(a, b, (((1,), (1,)), ((), ())), preferred_element_type=F32)


def dot_tn(a, b):
    return lax.dot_general(a, b, (((0,), (0,)), ((), ())), preferred_element_type=F32)


def rotary_rows():
    lane = np.arange(128) % HD
    freqs = (10000.0 ** (-np.arange(ROT // 2) * 2.0 / ROT)).astype(np.float32)
    angle = np.arange(SEQ_LEN, dtype=np.float32)[:, None] * freqs[lane % (ROT // 2)][None, :]
    turned = lane < ROT
    cos = np.where(turned, np.cos(angle), 1.0)
    sin = np.where(turned, np.sin(angle) * np.where(lane < ROT // 2, -1.0, 1.0), 0.0)
    return np.stack([cos, sin]).astype(np.float32)


def turn(values, cos, sin):
    lane = lax.broadcasted_iota(jnp.int32, values.shape, 1)
    first = lax.rem(lane, HD) < ROT // 2
    partner = jnp.where(first, pltpu.roll(values, 240, 1), pltpu.roll(values, 16, 1))
    return values * cos + partner * sin


def tables(tab, rows):
    cos, sin = tab[0, rows, :], tab[1, rows, :]
    return jnp.concatenate([cos, cos], axis=1), jnp.concatenate([sin, sin], axis=1)


def head_lanes(h, rows):
    lane = lax.broadcasted_iota(jnp.int32, (rows, 256), 1)
    return lax.div(lane, HD) == h


RB = 256


def rows_of(i):
    return pl.ds(pl.multiple_of(i * RB, RB), RB)


def project(i, n, wa, bias, tab, q, k, v, a, dh):
    rows = rows_of(i)
    cos, sin = tables(tab, rows)
    joined = dot_nn(n[rows, :], wa[...]) + bias[0:1, :]
    q[rows, :] = (turn(joined[:, :256], cos, sin) * HD**-0.5).astype(BF16)
    k[rows, :] = turn(joined[:, 256:512], cos, sin).astype(BF16)
    v[rows, :] = joined[:, 512:768].astype(BF16)
    z = joined[:, 768:]
    z2 = z * z
    th = jnp.tanh(z * (GELU + (GELU * 0.044715) * z2))
    half = 0.5 + 0.5 * th
    a[rows, 256:] = (z * half).astype(BF16)
    dh[rows, 768:] = (half + (half - half * half) * z * (2 * GELU + (6 * GELU * 0.044715) * z2)).astype(BF16)


def attend(i, q, k, v, a, lse):
    rows, before = slice(i * RB, (i + 1) * RB), i * RB
    qb = q[rows, :]
    causal = lax.broadcasted_iota(jnp.int32, (RB, RB), 1) <= lax.broadcasted_iota(jnp.int32, (RB, RB), 0)
    lane = lax.broadcasted_iota(jnp.int32, (RB, 128), 1)
    context = jnp.zeros((RB, 256), F32)
    logs = jnp.zeros((RB, 128), F32)
    for h in range(4):
        mine = head_lanes(h, RB)
        qh = jnp.where(mine, qb, jnp.zeros_like(qb))
        s1 = jnp.where(causal, dot_nt(qh, k[rows, :]), -1e30)
        top = jnp.max(s1, axis=1, keepdims=True)
        if i:
            s0 = dot_nt(qh, k[:before, :])
            top = jnp.maximum(top, jnp.max(s0, axis=1, keepdims=True))
        p1 = jnp.exp(s1 - top)
        total = jnp.sum(p1, axis=1, keepdims=True)
        out = dot_nn(p1.astype(BF16), v[rows, :])
        if i:
            p0 = jnp.exp(s0 - top)
            total = total + jnp.sum(p0, axis=1, keepdims=True)
            out = out + dot_nn(p0.astype(BF16), v[:before, :])
        context = jnp.where(mine, out / total, context)
        logs = jnp.where(lane == h, top + jnp.log(total), logs)
    a[rows, :256] = context.astype(BF16)
    lse[rows, :] = logs


def attend_back(i, q, k, v, lse, tab, dh, dk, dv, ps, ds):
    rows, width = slice(i * RB, (i + 1) * RB), (i + 1) * RB
    qb, gb = q[rows, :], dh[rows, :256]
    causal = lax.broadcasted_iota(jnp.int32, (RB, RB), 1) <= lax.broadcasted_iota(jnp.int32, (RB, RB), 0)
    dq = jnp.zeros((RB, 256), F32)
    for h in range(4):
        mine = head_lanes(h, RB)
        part = slice(h * RB, (h + 1) * RB)
        qh = jnp.where(mine, qb, jnp.zeros_like(qb))
        gh = jnp.where(mine, gb, jnp.zeros_like(gb))
        ps[part, SEQ_LEN:] = qh
        ds[part, SEQ_LEN : SEQ_LEN + 256] = gh
        log = lse[rows, h : h + 1]
        s = dot_nt(qh, k[:width, :])
        if i:
            s = jnp.concatenate([s[:, : i * RB], jnp.where(causal, s[:, i * RB :], -1e30)], axis=1)
        else:
            s = jnp.where(causal, s, -1e30)
        p = jnp.exp(s - log)
        t = p * dot_nt(gh, v[:width, :])
        row = jnp.sum(t, axis=1, keepdims=True)
        low = (t - p * row).astype(BF16)
        ps[part, :width] = p.astype(BF16)
        ds[part, :width] = low
        dq = jnp.where(mine, dot_nn(low, k[:width, :]), dq)
    key = dot_tn(ds[:, :width], ps[:, SEQ_LEN:])
    val = dot_tn(ps[:, :width], ds[:, SEQ_LEN : SEQ_LEN + 256])
    if i == 3:
        dk[...] = key
        dv[...] = val
    else:
        dk[:width, :] += key
        dv[:width, :] += val
    cos, sin = tables(tab, rows)
    dh[rows, :256] = turn(dq * HD**-0.5, cos, -sin).astype(BF16)


def keys_back(tab, dh, dk, dv):
    @pl.loop(0, 4)
    def _(i):
        rows = rows_of(i)
        cos, sin = tables(tab, rows)
        dh[rows, 256:512] = turn(dk[rows, :], cos, -sin).astype(BF16)
        dh[rows, 512:768] = dv[rows, :].astype(BF16)


def branch_out(i, a, wb, o):
    rows = rows_of(i)
    o[rows, :] = dot_nn(a[rows, :], wb[...]).astype(BF16)


def branch_back(i, g, wb, dh):
    rows = rows_of(i)
    back = dot_nt(g[rows, :], wb[...])
    dh[rows, :256] = back[:, :256].astype(BF16)
    dh[rows, 768:] = (back[:, 256:] * dh[rows, 768:].astype(F32)).astype(BF16)


def columns_of(m):
    return pl.ds(pl.multiple_of(m * 256, 256), 256)


def grad_wb(m, a, g, wb):
    cols = columns_of(m)
    wb[:, cols] = dot_tn(a[...], g[:, cols]).astype(BF16)


def normed_back(i, dh, wa, out):
    rows = rows_of(i)
    out[rows, :] = dot_nt(dh[rows, :], wa[...]).astype(BF16)


def grad_wa(m, n, dh, wa):
    cols = columns_of(m)
    wa[cols, :] = dot_tn(n[:, cols], dh[...]).astype(BF16)


def grad_bias(dh, put):
    total = jnp.sum(dh[0:RB, :].astype(F32), axis=0, keepdims=True)
    for i in range(1, 4):
        total = total + jnp.sum(dh[i * RB : (i + 1) * RB, :].astype(F32), axis=0, keepdims=True)
    for j in range(WA // 128):
        put(j, total[:, j * 128 : (j + 1) * 128])


def row_block(ref):
    return lambda i: ref.at[pl.ds(pl.multiple_of(i * TOK, TOK), TOK)]


def row_half(ref):
    return lambda i, h: ref.at[pl.ds(pl.multiple_of(i * TOK + h * (TOK // 2), TOK // 2), TOK // 2)]


def col_block(ref):
    return lambda i: ref.at[:, pl.ds(pl.multiple_of(i * 128, 128), 128)]


def col_half(ref):
    return lambda i, h: ref.at[pl.ds(h * (WB // 2), WB // 2), pl.ds(pl.multiple_of(i * 128, 128), 128)]


def sixteen_rows(i):
    return pl.ds(pl.multiple_of(i * 16, 16), 16)


def load_rows(src, dst, sem):
    copies = [pltpu.make_async_copy(src.at[pl.ds(j * 64, 64)], dst.at[j], sem.at[j]) for j in range(2)]
    for copy in copies:
        copy.start()
    return copies


def loaded(ref, i):
    return ref[lax.div(i, 4), pl.ds(pl.multiple_of(lax.rem(i, 4) * 16, 16), 16), :].astype(F32)


def block_kernel(x_ref, cot_ref, gain_ref, shift_ref, dense_b, down_b, qkv_ref, up_ref, dense_ref, down_ref, qkv_b, up_b, tab_ref,
                 out_ref, ig_ref, vec_out, dqkv_out, dup_out, ddense_out, ddown_out, db_out, xhats,
                 n, g, wa, wb, vecs, bias, o, q, k, v, a, dh, lse, dk, dv, tab,
                 sib_a, sib_b, far_a, near_a, pair_a, far_b, near_b, pair_b, far_o, near_o, pair_o, far_n, near_n, pair_n,
                 part, v1, v2, dbs, ssem, rsem, v0s, v0r, v1s, v1r, v2s, v2r, dss, dsr, lsem):
    f, t = lax.axis_index("fsdp"), lax.axis_index("tp")
    tp, fs = Group("tp"), Group("fsdp")
    wa_own, wb_own = row_block(wa)(f), col_block(wb)(f)
    vec_slot = col_block(vecs)
    own = [pltpu.make_async_copy(x_ref, row_block(o)(t), lsem.at[0])]
    for j in range(3):
        own.append(pltpu.make_async_copy(qkv_ref.at[j], wa_own.at[:, pl.ds(j * 256, 256)], lsem.at[1 + j]))
    own += [
        pltpu.make_async_copy(up_ref, wa_own.at[:, pl.ds(768, 1024)], lsem.at[4]),
        pltpu.make_async_copy(dense_ref, wb_own.at[pl.ds(0, 256)], lsem.at[5]),
        pltpu.make_async_copy(down_ref, wb_own.at[pl.ds(256, 1024)], lsem.at[6]),
        pltpu.make_async_copy(cot_ref, row_block(g)(t), lsem.at[7]),
        pltpu.make_async_copy(tab_ref, tab, lsem.at[8]),
    ]
    for copy in own:
        copy.start()
    f32_row = lambda ref: ref[...].astype(F32).reshape(1, ref.shape[0])
    rows = [f32_row(gain_ref), f32_row(shift_ref), f32_row(dense_b) + f32_row(down_b), jnp.zeros((5, 128), F32)]
    vecs[:, pl.ds(pl.multiple_of(f * 128, 128), 128)] = jnp.concatenate(rows, axis=0)
    for j in range(3):
        bias[0:1, j * 256 : (j + 1) * 256] = qkv_b[j : j + 1, :].astype(F32)
    bias[0:1, 768:] = f32_row(up_b)
    ga = Gather(fs, row_block(wa), row_half(wa), ssem.at[0], rsem.at[0], sibling=True)
    gb = Gather(fs, col_block(wb), col_half(wb), ssem.at[1], rsem.at[1], sibling=True)
    gn = Gather(tp, row_block(o), row_half(o), ssem.at[2], rsem.at[2])
    gg = Gather(tp, row_block(g), row_half(g), ssem.at[3], rsem.at[3])
    so = Scatter(tp, row_block(o), row_half(o), far_o, near_o, pair_o, ssem.at[4], rsem.at[4], 16)
    sn = Scatter(tp, row_block(g), row_half(g), far_n, near_n, pair_n, ssem.at[5], rsem.at[5], 16)
    sa = Scatter(fs, row_block(wa), row_half(wa), far_a, near_a, pair_a, ssem.at[6], rsem.at[6], 16, sib_a)
    sb = Scatter(fs, col_block(wb), col_half(wb), far_b, near_b, pair_b, ssem.at[7], rsem.at[7], 128, sib_b)

    def normalize(r, k):
        block = r * 4 + k
        parked = (near_o if r is tp.r else near_n).at[lax.div(k, 2), lax.rem(k, 2)]

        @pl.loop(0, 2)
        def _(i):
            rows = pl.ds(pl.multiple_of(block * TOK + i * 64, 64), 64)
            xf = o[rows, :].astype(F32)
            centered = xf - jnp.mean(xf, axis=-1, keepdims=True)
            variance = jnp.mean(centered * centered, axis=-1, keepdims=True)
            xhat = centered * lax.rsqrt(variance + EPS)
            n[rows, :] = (xhat * vecs[0:1, :] + vecs[1:2, :]).astype(BF16)
            parked[pl.ds(pl.multiple_of(i * 64, 64), 64), :] = xhat.astype(BF16)

    greet(all_peers(f, t))
    own[0].wait()
    gn.ring(0)
    for d in range(1, 16):
        remote(vec_slot(f), vec_slot(f), v0s.at[d], v0r.at[d], (lax.rem(f + d, 16), t)).start()
    gn.pair_send()
    for copy in own[1:5]:
        copy.wait()
    ga.ring(0)
    for copy in own[5:]:
        copy.wait()
    gn.forward(0)
    for d in range(1, 16):
        source = lax.rem(f + 16 - d, 16)
        remote(vec_slot(source), vec_slot(source), v0s.at[d], v0r.at[d], (source, t)).wait_recv()
    normalize(tp.r, tp.k)
    ga.forward(0)
    gb.ring(0)
    gn.pair_recv()
    ga.pair_send()
    ga.near(0)
    normalize(tp.other, tp.k)
    gn.near(0)
    normalize(tp.r, tp.down)
    normalize(tp.r, tp.up)
    gb.forward(0)
    ga.pair_recv()
    gb.pair_send()
    gg.pair_send()
    gn.forward(1)
    gn.far(0)
    gg.ring(0)
    part[...] = jnp.zeros_like(part)

    @pl.loop(0, TOK // 16)
    def _(i):
        cot = g[pl.ds(pl.multiple_of(t * TOK + i * 16, 16), 16), :].astype(F32)
        part[16:24, :] += cot[:8] + cot[8:]

    normalize(tp.r, tp.far)
    ga.far(0)
    ga.forward(1)
    gn.near(1)
    normalize(tp.other, tp.down)
    normalize(tp.other, tp.up)
    gb.near(0)
    gb.pair_recv()
    ga.near(1)
    gn.far(1)
    normalize(tp.other, tp.far)
    keep = [pltpu.make_async_copy(ref, xhats.at[i], lsem.at[9 + i]) for i, ref in enumerate((near_o, near_n))]
    for copy in keep:
        copy.start()
    ga.far(1)
    ga.finish()
    project(0, n, wa, bias, tab, q, k, v, a, dh)
    gg.forward(0)
    gb.far(0)
    gb.forward(1)
    project(1, n, wa, bias, tab, q, k, v, a, dh)
    gg.pair_recv()
    project(2, n, wa, bias, tab, q, k, v, a, dh)
    gb.near(1)
    project(3, n, wa, bias, tab, q, k, v, a, dh)
    gn.sent()
    attend(0, q, k, v, a, lse)
    attend(1, q, k, v, a, lse)
    gg.near(0)
    gb.far(1)
    attend(2, q, k, v, a, lse)
    attend(3, q, k, v, a, lse)
    gb.finish()
    side = lax.div(tp.far, 2)
    halves = (tp.other * 2 + side, tp.r * 2 + side, tp.other * 2 + 1 - side, tp.r * 2 + 1 - side)
    for copy in keep:
        copy.wait()
    branch_out(halves[0], a, wb, o)
    gg.forward(1)

    @pl.loop(1, 4)
    def _(i):
        step = jnp.where(i == 1, halves[1], jnp.where(i == 2, halves[2], halves[3]))
        branch_out(step, a, wb, o)

    gg.far(0)
    branch_back(tp.r * 2, g, wb, dh)
    branch_back(tp.r * 2 + 1, g, wb, dh)
    gg.near(1)
    gg.far(1)
    so.far(0)
    so.far(1)
    gg.finish()
    branch_back(tp.other * 2, g, wb, dh)
    branch_back(tp.other * 2 + 1, g, wb, dh)
    so.free(0)
    for s in range(8):
        grad_wb(sb.chip(s), a, g, wb)
        sb.sib_send(s)
        if s > 1:
            sb.sib_add(s - 2)
        if s == 2:
            sb.far(0)
        if s == 3:
            sb.far(1)
        if s == 4:
            so.relay(0)
            so.free(1)
        if s == 5:
            sb.free(0)
    sb.sib_add(6)
    sb.sib_add(7)
    sb.free(1)
    so.relay(1)
    for i in (3, 2, 1, 0):
        attend_back(i, q, k, v, lse, tab, dh, dk, dv, a, g)
        if i == 3:
            sb.relay(0)
        if i == 2:
            sb.relay(1)

    def fetch(j):
        place, sem = (j % 2) * 2 * RB, (j % 2) * 4
        src = xhats.at[1 - j % 2, side if j < 2 else 1 - side]
        copies = []
        for half in range(2):
            for i in range(2):
                dst = a.at[pl.ds(place + half * RB + i * TOK, TOK), pl.ds(0, 1024)]
                piece_in = src.at[i, :, pl.ds(half * 1024, 1024)]
                copies.append(pltpu.make_async_copy(piece_in, dst, lsem.at[29 + sem + half * 2 + i]))
        for copy in copies:
            copy.start()
        return copies

    def norm_sums(j):
        place, first = (j % 2) * 2 * RB, halves[j] * RB

        @pl.loop(0, RB // 64)
        def _(i):
            rows = pl.ds(pl.multiple_of(first + i * 64, 64), 64)
            for half in range(2):
                cols = slice(half * 1024, half * 1024 + 1024)
                grad = g[rows, cols].astype(F32)
                xhat = a[pl.ds(pl.multiple_of(place + half * RB + i * 64, 64), 64), 0:1024].astype(F32)
                part[0:8, cols] += jnp.sum((grad * xhat).reshape(8, 8, 1024), axis=0)
                part[8:16, cols] += jnp.sum(grad.reshape(8, 8, 1024), axis=0)

    fetched = [fetch(0), fetch(1)]
    keys_back(tab, dh, dk, dv)
    for j in range(4):
        normed_back(halves[j], dh, wa, g)
        if j < 2:
            sn.far(j)
        for copy in fetched[j]:
            copy.wait()
        norm_sums(j)
        if j < 2:
            fetched.append(fetch(j + 2))
        if j == 1:
            so.pair()
            sb.pair()
    sn.free(0)
    for row in range(3):
        part[24 + row : 25 + row, :] = jnp.sum(part[row * 8 : row * 8 + 8, :], axis=0, keepdims=True)
    piece = lambda i: part.at[pl.ds(24, 8), pl.ds(pl.multiple_of(i * 128, 128), 128)]
    for d in range(1, 16):
        to = lax.rem(f + d, 16)
        remote(piece(to), v1.at[f], v1s.at[d], v1r.at[d], (to, t)).start()
    v1[f] = part[24:, pl.ds(pl.multiple_of(f * 128, 128), 128)]

    for s in range(8):
        grad_wa(sa.chip(s), n, dh, wa)
        sa.sib_send(s)
        if s > 1:
            sa.sib_add(s - 2)
        if s == 2:
            sa.far(0)
        if s == 3:
            sa.far(1)
            sn.relay(0)
            sn.free(1)
        if s == 5:
            sa.free(0)
    sa.sib_add(6)
    sa.sib_add(7)
    sa.free(1)

    def put(j, row):
        dbs[f, j : j + 1, :] = row

    grad_bias(dh, put)
    dbs[f, WA // 128 :, :] = jnp.zeros((16 - WA // 128, 128), F32)
    for d in range(1, 16):
        remote(dbs.at[f], dbs.at[f], dss.at[d], dsr.at[d], (lax.rem(f + d, 16), t)).start()
    for d in range(1, 16):
        source = lax.rem(f + 16 - d, 16)
        remote(piece(source), v1.at[source], v1s.at[d], v1r.at[d], (source, t)).wait_recv()
    v2[t] = jnp.sum(v1[...], axis=0)
    for d in range(1, 8):
        remote(v2.at[t], v2.at[t], v2s.at[d], v2r.at[d], (f, lax.rem(t + d, 8))).start()
    sn.relay(1)
    sa.relay(0)
    out_refs = so.last()
    rows_in = load_rows(x_ref, far_o.at[1], lsem.at[pl.ds(27, 2)])
    for copy in rows_in:
        copy.wait()

    @pl.loop(0, TOK // 16)
    def _(i):
        rows = sixteen_rows(i)
        total = loaded(far_o.at[1], i) + vecs[2:3, :]
        for ref in out_refs:
            total = total + ref[rows, :].astype(F32)
        pair_o[rows, :] = total.astype(BF16)

    results = [pltpu.make_async_copy(pair_o, out_ref, lsem.at[14])]
    results[0].start()
    cots = load_rows(cot_ref, far_o.at[0], lsem.at[pl.ds(25, 2)])

    sa.relay(1)
    sb_refs = sb.last()
    dense_sum, down_sum = dk.at[pl.ds(0, 256), pl.ds(128, 128)], dk.at[:, pl.ds(0, 128)]
    add_rows(dense_sum, [ref.at[pl.ds(0, 256)] for ref in sb_refs], 128)
    add_rows(down_sum, [ref.at[pl.ds(256, 1024)] for ref in sb_refs], 128)
    results.append(pltpu.make_async_copy(dense_sum, ddense_out, lsem.at[15]))
    results.append(pltpu.make_async_copy(down_sum, ddown_out, lsem.at[16]))
    results[1].start()
    results[2].start()
    sn.pair()
    sa.pair()
    for d in range(1, 16):
        source = lax.rem(f + 16 - d, 16)
        remote(dbs.at[source], dbs.at[source], dss.at[d], dsr.at[d], (source, t)).wait_recv()
    db_out[...] = jnp.sum(dbs[...], axis=0)
    for d in range(1, 8):
        source = lax.rem(t + 8 - d, 8)
        remote(v2.at[source], v2.at[source], v2s.at[d], v2r.at[d], (f, source)).wait_recv()
    vec_out[...] = jnp.sum(v2[...], axis=0)
    for copy in cots:
        copy.wait()
    n_refs = sn.last()

    @pl.loop(0, 2)
    def _(i):
        rows = pl.ds(pl.multiple_of(i * 64, 64), 64)
        xf = far_o[1, i].astype(F32)
        centered = xf - jnp.mean(xf, axis=-1, keepdims=True)
        inv = lax.rsqrt(jnp.mean(centered * centered, axis=-1, keepdims=True) + EPS)
        xhat = centered * inv
        total = n_refs[0][rows, :].astype(F32)
        for ref in n_refs[1:]:
            total = total + ref[rows, :].astype(F32)
        e = total * vecs[0:1, :]
        back = (e - jnp.mean(e, axis=-1, keepdims=True) - xhat * jnp.mean(e * xhat, axis=-1, keepdims=True)) * inv
        pair_n[rows, :] = (far_o[0, i].astype(F32) + back).astype(BF16)

    results.append(pltpu.make_async_copy(pair_n, ig_ref, lsem.at[17]))
    results[3].start()
    sa_refs = sa.last()
    for j in range(7):
        here = dv.at[pl.ds(j * TOK, TOK)]
        add_rows(here, [ref.at[:, pl.ds(j * 256, 256)] for ref in sa_refs], TOK)
        there = dqkv_out.at[j] if j < 3 else dup_out.at[:, pl.ds((j - 3) * 256, 256)]
        results.append(pltpu.make_async_copy(here, there, lsem.at[18 + j]))
        results[-1].start()
    for copy in results:
        copy.wait()
    for op in (so, sn, sa, sb):
        op.sent()
    for d in range(1, 16):
        to = lax.rem(f + d, 16)
        remote(vec_slot(f), vec_slot(f), v0s.at[d], v0r.at[d], (to, t)).wait_send()
        remote(dbs.at[f], dbs.at[f], dss.at[d], dsr.at[d], (to, t)).wait_send()
        remote(piece(to), v1.at[f], v1s.at[d], v1r.at[d], (to, t)).wait_send()
    for d in range(1, 8):
        remote(v2.at[t], v2.at[t], v2s.at[d], v2r.at[d], (f, lax.rem(t + d, 8))).wait_send()


def run_block(*operands):
    def bufs(full, half):
        return [pltpu.VMEM((2, 2) + half, BF16), pltpu.VMEM((2, 2) + full, BF16), pltpu.VMEM(full, BF16)]

    dma = pltpu.SemaphoreType.DMA
    sds = jax.ShapeDtypeStruct
    return pl.pallas_call(
        block_kernel,
        out_shape=(
            sds((TOK, D), BF16),
            sds((TOK, D), BF16),
            sds((8, 128), F32),
            sds((3, TOK, 256), F32),
            sds((TOK, 1024), F32),
            sds((256, 128), F32),
            sds((1024, 128), F32),
            sds((16, 128), F32),
            sds((2, 2, 2, TOK, D), BF16),
        ),
        in_specs=[ANY, ANY, VMEM, VMEM, VMEM, VMEM, ANY, ANY, ANY, ANY, VMEM, VMEM, ANY],
        out_specs=(ANY, ANY, VMEM, ANY, ANY, ANY, ANY, VMEM, ANY),
        scratch_shapes=[
            pltpu.VMEM((SEQ_LEN, D), BF16),
            pltpu.VMEM((SEQ_LEN, D), BF16),
            pltpu.VMEM((D, WA), BF16),
            pltpu.VMEM((WB, D), BF16),
            pltpu.VMEM((8, D), F32),
            pltpu.VMEM((1, WA), F32),
            pltpu.VMEM((SEQ_LEN, D), BF16),
            pltpu.VMEM((SEQ_LEN, 256), BF16),
            pltpu.VMEM((SEQ_LEN, 256), BF16),
            pltpu.VMEM((SEQ_LEN, 256), BF16),
            pltpu.VMEM((SEQ_LEN, WB), BF16),
            pltpu.VMEM((SEQ_LEN, WA), BF16),
            pltpu.VMEM((SEQ_LEN, 128), F32),
            pltpu.VMEM((SEQ_LEN, 256), F32),
            pltpu.VMEM((SEQ_LEN, 256), F32),
            pltpu.VMEM((2, SEQ_LEN, 128), F32),
            pltpu.VMEM((8, TOK, WA), BF16),
            pltpu.VMEM((8, WB, 128), BF16),
            *bufs((TOK, WA), (TOK // 2, WA)),
            *bufs((WB, 128), (WB // 2, 128)),
            *bufs((TOK, D), (TOK // 2, D)),
            *bufs((TOK, D), (TOK // 2, D)),
            pltpu.VMEM((32, D), F32),
            pltpu.VMEM((16, 8, 128), F32),
            pltpu.VMEM((8, 8, 128), F32),
            pltpu.VMEM((16, 16, 128), F32),
            dma((8, 21)), dma((8, 21)),
            dma((16,)), dma((16,)), dma((16,)), dma((16,)), dma((8,)), dma((8,)), dma((16,)), dma((16,)), dma((37,)),
        ],
        compiler_params=pltpu.CompilerParams(collective_id=0, has_side_effects=True, vmem_limit_bytes=64 * 2**20 - 2**18),
        name="block_all",
    )(*operands)


def give_kernel(out_in, ig_in, dqkv_in, dup_in, ddense_in, ddown_in, vec, db,
                out, ig, gain, shift, dqkv, qkv_b, ddense, dense_b, dup, up_b, ddown, down_b, sem):
    pairs = [(out_in, out), (ig_in, ig), (dqkv_in, dqkv), (dup_in, dup), (ddense_in, ddense), (ddown_in, ddown)]
    copies = [pltpu.make_async_copy(src, dst, sem.at[i]) for i, (src, dst) in enumerate(pairs)]
    for copy in copies:
        copy.start()
    gain[...] = vec[0, :]
    shift[...] = vec[1, :]
    dense_b[...] = vec[2, :]
    down_b[...] = vec[2, :]
    for j in range(6):
        qkv_b[j // 2 : j // 2 + 1, (j % 2) * 128 : (j % 2) * 128 + 128] = db[j : j + 1, :]
    for j in range(8):
        up_b[pl.ds(j * 128, 128)] = db[6 + j, :]
    for copy in copies:
        copy.wait()


def give(*results):
    sds = jax.ShapeDtypeStruct
    return pl.pallas_call(
        give_kernel,
        out_shape=(
            sds((TOK, D), BF16),
            sds((TOK, D), BF16),
            sds((128,), F32),
            sds((128,), F32),
            sds((3, TOK, 256), F32),
            sds((3, 256), F32),
            sds((256, 128), F32),
            sds((128,), F32),
            sds((TOK, 1024), F32),
            sds((1024,), F32),
            sds((1024, 128), F32),
            sds((128,), F32),
        ),
        in_specs=[VMEM] * 8,
        out_specs=(ANY, ANY, VMEM, VMEM, ANY, VMEM, ANY, VMEM, ANY, VMEM, ANY, VMEM),
        scratch_shapes=[pltpu.SemaphoreType.DMA((6,))],
        compiler_params=pltpu.CompilerParams(vmem_limit_bytes=60 * 2**20),
        name="give",
    )(*results)


def on_device(
    block_input, norm_gain, norm_bias, qkv_weight, qkv_bias, dense_weight, dense_bias, up_weight, up_bias,
    down_weight, down_bias, cotangent,
):
    out, ig, vec, dqkv, dup, ddense, ddown, db, _ = run_block(
        block_input, cotangent, norm_gain, norm_bias, dense_bias, down_bias, jnp.transpose(qkv_weight, (1, 0, 2)),
        up_weight, dense_weight, down_weight, qkv_bias, up_bias, jnp.asarray(rotary_rows()),
    )
    results = list(give(out, ig, dqkv, dup, ddense, ddown, vec, db))
    results[4] = jnp.transpose(results[4], (1, 0, 2))
    return tuple(results)


def solution(mesh):
    in_specs = (
        P(("fsdp", "tp"), None),
        P("fsdp"),
        P("fsdp"),
        P("fsdp", None, "tp"),
        P(None, "tp"),
        P("tp", "fsdp"),
        P("fsdp"),
        P("fsdp", "tp"),
        P("tp"),
        P("tp", "fsdp"),
        P("fsdp"),
        P(("fsdp", "tp"), None),
    )
    out_specs = (
        P(("fsdp", "tp"), None),
        P(("fsdp", "tp"), None),
        P("fsdp"),
        P("fsdp"),
        P("fsdp", None, "tp"),
        P(None, "tp"),
        P("tp", "fsdp"),
        P("fsdp"),
        P("fsdp", "tp"),
        P("tp"),
        P("tp", "fsdp"),
        P("fsdp"),
    )
    return jax.shard_map(
        on_device, mesh=mesh, in_specs=in_specs, out_specs=out_specs, check_vma=False
    )
```

profile of v0, /device:TPU:0, one launch (start us, length us, event | category | flops | bytes accessed | tf_op | source)
XLA Modules:
  0.0 179.9 jit_solution(17072795052850477638)
XLA Ops:
  0.6 174.9 %block_all.1 = (bf16[128,2048]{1,0:T(8,128)(2,1)}, bf16[128,2048]{1,0:T(8,128)(2,1)}, f32[8,128]{1,0:T(8,128)}, f32[3,128,256]{2,1,0:T(8,128)}, f32[128,1024]{1,...) custom-call(bf16[128,2048]{1,0:T(8,128)(2,1)} %x_ref.1, ...), custom_call_target="tpu_custom_call" | custom-call | tf_op jit(solution)/shard_map/block_all/pallas_call | solution.py:766
  175.6 3.8 %give.1 = (bf16[128,2048]{1,0:T(8,128)(2,1)}, bf16[128,2048]{1,0:T(8,128)(2,1)}, f32[128]{0:T(128)}, f32[128]{0:T(128)}, f32[3,128,256]{2,1,0:T(8,128)}, /*index...) custom-call(bf16[128,2048]{1,0:T(8,128)(2,1)} %get-tuple-element.32., ...), custom_call_target="tpu_custom_call" | custom-call | tf_op jit(solution)/shard_map/give/pallas_call | solution.py:836
where the time goes:
time: 183 us; the launch traced here: 180 us
  Pallas kernels  179 us (98%)
    pallas_call x1, Pallas kernels, run_block(): pl.pallas_call(block_kernel, out_shape=(sds((TOK, D), BF16), sds((TOK, D)...  175 us
    pallas_call x1, Pallas kernels, give(): pl.pallas_call(give_kernel, out_shape=(sds((TOK, D), BF16), sds((TOK, D),...  3.84 us

commit v1 on v0

--- a/solution.py
+++ b/solution.py
@@ -149,6 +149,13 @@
         self.sent()
 
 
+def pick(i, values):
+    out = values[0]
+    for j, value in enumerate(values[1:], 1):
+        out = jnp.where(i == j, value, out)
+    return out
+
+
 def add_rows(out, ins, chunk):
     @pl.loop(0, out.shape[0] // chunk)
     def _(i):
@@ -189,15 +196,15 @@
                 add(13 + s, block(g.index(r, k, 1 - g.c)), sib.at[s], g.sib)
 
     def chip(self, s):
-        r, k = self.order[s]
-        return k * 2 + r
-
-    def sib_send(self, s):
-        self.send(13 + s)
+        return pick(s, [k * 2 + r for r, k in self.order])
+
+    def sib_copy(self, s):
+        src, dst = self.block(self.chip(s) * 2 + 1 - self.g.c), self.sib_ref.at[s]
+        return remote(src, dst, self.ssem.at[13 + s], self.rsem.at[13 + s], self.g.sib)
 
     def sib_add(self, s):
-        self.recv(13 + s)
-        mine = self.block(self.g.index(*self.order[s]))
+        self.sib_copy(s).wait_recv()
+        mine = self.block(self.chip(s) * 2 + self.g.c)
         add_rows(mine, [mine, self.sib_ref.at[s]], self.chunk)
 
     def far(self, row):
@@ -535,15 +542,25 @@
         copy.start()
     ga.far(1)
     ga.finish()
-    project(0, n, wa, bias, tab, q, k, v, a, dh)
-    gg.forward(0)
-    gb.far(0)
-    gb.forward(1)
-    project(1, n, wa, bias, tab, q, k, v, a, dh)
-    gg.pair_recv()
-    project(2, n, wa, bias, tab, q, k, v, a, dh)
-    gb.near(1)
-    project(3, n, wa, bias, tab, q, k, v, a, dh)
+
+    @pl.loop(0, 4)
+    def _(i):
+        project(i, n, wa, bias, tab, q, k, v, a, dh)
+
+        @pl.when(i == 0)
+        def _():
+            gg.forward(0)
+            gb.far(0)
+            gb.forward(1)
+
+        @pl.when(i == 1)
+        def _():
+            gg.pair_recv()
+
+        @pl.when(i == 2)
+        def _():
+            gb.near(1)
+
     gn.sent()
     attend(0, q, k, v, a, lse)
     attend(1, q, k, v, a, lse)
@@ -556,39 +573,57 @@
     halves = (tp.other * 2 + side, tp.r * 2 + side, tp.other * 2 + 1 - side, tp.r * 2 + 1 - side)
     for copy in keep:
         copy.wait()
-    branch_out(halves[0], a, wb, o)
-    gg.forward(1)
-
-    @pl.loop(1, 4)
+
+    @pl.loop(0, 4)
     def _(i):
-        step = jnp.where(i == 1, halves[1], jnp.where(i == 2, halves[2], halves[3]))
-        branch_out(step, a, wb, o)
+        branch_out(pick(i, halves), a, wb, o)
+
+        @pl.when(i == 0)
+        def _():
+            gg.forward(1)
 
     gg.far(0)
-    branch_back(tp.r * 2, g, wb, dh)
-    branch_back(tp.r * 2 + 1, g, wb, dh)
-    gg.near(1)
-    gg.far(1)
-    so.far(0)
-    so.far(1)
+
+    @pl.loop(0, 4)
+    def _(i):
+        @pl.when(i == 2)
+        def _():
+            gg.near(1)
+            gg.far(1)
+            so.far(0)
+            so.far(1)
+
+        branch_back(jnp.where(i < 2, tp.r * 2 + i, tp.other * 2 + i - 2), g, wb, dh)
+
     gg.finish()
-    branch_back(tp.other * 2, g, wb, dh)
-    branch_back(tp.other * 2 + 1, g, wb, dh)
     so.free(0)
-    for s in range(8):
+
+    @pl.loop(0, 8)
+    def _(s):
         grad_wb(sb.chip(s), a, g, wb)
-        sb.sib_send(s)
-        if s > 1:
+        sb.sib_copy(s).start()
+
+        @pl.when(s > 1)
+        def _():
             sb.sib_add(s - 2)
-        if s == 2:
+
+        @pl.when(s == 2)
+        def _():
             sb.far(0)
-        if s == 3:
+
+        @pl.when(s == 3)
+        def _():
             sb.far(1)
-        if s == 4:
+
+        @pl.when(s == 4)
+        def _():
             so.relay(0)
             so.free(1)
-        if s == 5:
+
+        @pl.when(s == 5)
+        def _():
             sb.free(0)
+
     sb.sib_add(6)
     sb.sib_add(7)
     sb.free(1)
@@ -601,20 +636,19 @@
             sb.relay(1)
 
     def fetch(j):
-        place, sem = (j % 2) * 2 * RB, (j % 2) * 4
-        src = xhats.at[1 - j % 2, side if j < 2 else 1 - side]
+        turn_, sem = lax.rem(j, 2), lax.rem(j, 2) * 4
+        place = turn_ * 2 * RB
+        src = xhats.at[1 - turn_, jnp.where(j < 2, side, 1 - side)]
         copies = []
         for half in range(2):
             for i in range(2):
-                dst = a.at[pl.ds(place + half * RB + i * TOK, TOK), pl.ds(0, 1024)]
+                dst = a.at[pl.ds(pl.multiple_of(place + half * RB + i * TOK, TOK), TOK), pl.ds(0, 1024)]
                 piece_in = src.at[i, :, pl.ds(half * 1024, 1024)]
                 copies.append(pltpu.make_async_copy(piece_in, dst, lsem.at[29 + sem + half * 2 + i]))
-        for copy in copies:
-            copy.start()
         return copies
 
     def norm_sums(j):
-        place, first = (j % 2) * 2 * RB, halves[j] * RB
+        place, first = lax.rem(j, 2) * 2 * RB, pick(j, halves) * RB
 
         @pl.loop(0, RB // 64)
         def _(i):
@@ -626,20 +660,37 @@
                 part[0:8, cols] += jnp.sum((grad * xhat).reshape(8, 8, 1024), axis=0)
                 part[8:16, cols] += jnp.sum(grad.reshape(8, 8, 1024), axis=0)
 
-    fetched = [fetch(0), fetch(1)]
+    for j in range(2):
+        for copy in fetch(jnp.int32(j)):
+            copy.start()
     keys_back(tab, dh, dk, dv)
-    for j in range(4):
-        normed_back(halves[j], dh, wa, g)
-        if j < 2:
-            sn.far(j)
-        for copy in fetched[j]:
+
+    @pl.loop(0, 4)
+    def _(j):
+        normed_back(pick(j, halves), dh, wa, g)
+
+        @pl.when(j == 0)
+        def _():
+            sn.far(0)
+
+        @pl.when(j == 1)
+        def _():
+            sn.far(1)
+
+        for copy in fetch(j):
             copy.wait()
         norm_sums(j)
-        if j < 2:
-            fetched.append(fetch(j + 2))
-        if j == 1:
+
+        @pl.when(j < 2)
+        def _():
+            for copy in fetch(j + 2):
+                copy.start()
+
+        @pl.when(j == 1)
+        def _():
             so.pair()
             sb.pair()
+
     sn.free(0)
     for row in range(3):
         part[24 + row : 25 + row, :] = jnp.sum(part[row * 8 : row * 8 + 8, :], axis=0, keepdims=True)
@@ -649,19 +700,30 @@
         remote(piece(to), v1.at[f], v1s.at[d], v1r.at[d], (to, t)).start()
     v1[f] = part[24:, pl.ds(pl.multiple_of(f * 128, 128), 128)]
 
-    for s in range(8):
+
+    @pl.loop(0, 8)
+    def _(s):
         grad_wa(sa.chip(s), n, dh, wa)
-        sa.sib_send(s)
-        if s > 1:
+        sa.sib_copy(s).start()
+
+        @pl.when(s > 1)
+        def _():
             sa.sib_add(s - 2)
-        if s == 2:
+
+        @pl.when(s == 2)
+        def _():
             sa.far(0)
-        if s == 3:
+
+        @pl.when(s == 3)
+        def _():
             sa.far(1)
             sn.relay(0)
             sn.free(1)
-        if s == 5:
+
+        @pl.when(s == 5)
+        def _():
             sa.free(0)
+
     sa.sib_add(6)
     sa.sib_add(7)
     sa.free(1)

time: 183 us -> 175 us (0.956); the launches traced: 180 us -> 175 us
  Pallas kernels: 179 us -> 174 us
    pallas_call x1, Pallas kernels: 175 us -> 170 us  [run_block(): pl.pallas_call(block_kernel, out_shape=(sds((TOK, D), BF16), sds((TOK, D)...]
where the time goes in v1:
time: 175 us
  Pallas kernels  174 us (99%)
    pallas_call x1, Pallas kernels, run_block(): pl.pallas_call(block_kernel, out_shape=(sds((TOK, D), BF16), sds((TOK, D)...  170 us
    pallas_call x1, Pallas kernels, give(): pl.pallas_call(give_kernel, out_shape=(sds((TOK, D), BF16), sds((TOK, D),...  3.84 us

profile of v1, /device:TPU:0, one launch (start us, length us, event | category | flops | bytes accessed | tf_op | source)
XLA Modules:
  0.0 174.8 jit_solution(8636509763025955743)
XLA Ops:
  0.6 170.1 %block_all.1 = (bf16[128,2048]{1,0:T(8,128)(2,1)}, bf16[128,2048]{1,0:T(8,128)(2,1)}, f32[8,128]{1,0:T(8,128)}, f32[3,128,256]{2,1,0:T(8,128)}, f32[128,1024]{1,...) custom-call(bf16[128,2048]{1,0:T(8,128)(2,1)} %x_ref.1, ...), custom_call_target="tpu_custom_call" | custom-call | tf_op jit(solution)/shard_map/block_all/pallas_call | solution.py:828
  170.8 3.8 %give.1 = (bf16[128,2048]{1,0:T(8,128)(2,1)}, bf16[128,2048]{1,0:T(8,128)(2,1)}, f32[128]{0:T(128)}, f32[128]{0:T(128)}, f32[3,128,256]{2,1,0:T(8,128)}, /*index...) custom-call(bf16[128,2048]{1,0:T(8,128)(2,1)} %get-tuple-element.32., ...), custom_call_target="tpu_custom_call" | custom-call | tf_op jit(solution)/shard_map/give/pallas_call | solution.py:898

commit v2 on v1

--- a/solution.py
+++ b/solution.py
@@ -876,11 +876,17 @@
 
 
 def give_kernel(out_in, ig_in, dqkv_in, dup_in, ddense_in, ddown_in, vec, db,
-                out, ig, gain, shift, dqkv, qkv_b, ddense, dense_b, dup, up_b, ddown, down_b, sem):
-    pairs = [(out_in, out), (ig_in, ig), (dqkv_in, dqkv), (dup_in, dup), (ddense_in, ddense), (ddown_in, ddown)]
-    copies = [pltpu.make_async_copy(src, dst, sem.at[i]) for i, (src, dst) in enumerate(pairs)]
-    for copy in copies:
+                out, ig, gain, shift, dqkv, qkv_b, ddense, dense_b, dup, up_b, ddown, down_b,
+                out_v, ig_v, dqkv_v, dup_v, ddense_v, ddown_v, sem_in, sem_out):
+    ways = [(out_in, out_v, out), (ig_in, ig_v, ig), (dup_in, dup_v, dup), (ddown_in, ddown_v, ddown)]
+    ways += [(dqkv_in, dqkv_v, dqkv), (ddense_in, ddense_v, ddense)]
+    arrive = [pltpu.make_async_copy(src, mid, sem_in.at[i]) for i, (src, mid, _) in enumerate(ways)]
+    leave = [pltpu.make_async_copy(mid, dst, sem_out.at[i]) for i, (_, mid, dst) in enumerate(ways)]
+    for copy in arrive:
         copy.start()
+    for first, second in zip(arrive, leave):
+        first.wait()
+        second.start()
     gain[...] = vec[0, :]
     shift[...] = vec[1, :]
     dense_b[...] = vec[2, :]
@@ -889,7 +895,7 @@
         qkv_b[j // 2 : j // 2 + 1, (j % 2) * 128 : (j % 2) * 128 + 128] = db[j : j + 1, :]
     for j in range(8):
         up_b[pl.ds(j * 128, 128)] = db[6 + j, :]
-    for copy in copies:
+    for copy in leave:
         copy.wait()
 
 
@@ -911,9 +917,18 @@
             sds((1024, 128), F32),
             sds((128,), F32),
         ),
-        in_specs=[VMEM] * 8,
+        in_specs=[ANY] * 6 + [VMEM] * 2,
         out_specs=(ANY, ANY, VMEM, VMEM, ANY, VMEM, ANY, VMEM, ANY, VMEM, ANY, VMEM),
-        scratch_shapes=[pltpu.SemaphoreType.DMA((6,))],
+        scratch_shapes=[
+            pltpu.VMEM((TOK, D), BF16),
+            pltpu.VMEM((TOK, D), BF16),
+            pltpu.VMEM((3, TOK, 256), F32),
+            pltpu.VMEM((TOK, 1024), F32),
+            pltpu.VMEM((256, 128), F32),
+            pltpu.VMEM((1024, 128), F32),
+            pltpu.SemaphoreType.DMA((6,)),
+            pltpu.SemaphoreType.DMA((6,)),
+        ],
         compiler_params=pltpu.CompilerParams(vmem_limit_bytes=60 * 2**20),
         name="give",
     )(*results)

time: 175 us -> 175 us (level)
  no operation moved by 1% of the time
where the time goes in v2:
time: 175 us
  Pallas kernels  174 us (99%)
    pallas_call x1, Pallas kernels, run_block(): pl.pallas_call(block_kernel, out_shape=(sds((TOK, D), BF16), sds((TOK, D)...  170 us
    pallas_call x1, Pallas kernels, give(): pl.pallas_call(give_kernel, out_shape=(sds((TOK, D), BF16), sds((TOK, D),...  3.94 us

profile of v2, /device:TPU:0, one launch (start us, length us, event | category | flops | bytes accessed | tf_op | source)
XLA Modules:
  0.0 174.9 jit_solution(12233809295291682329)
XLA Ops:
  0.6 170.1 %block_all.1 = (bf16[128,2048]{1,0:T(8,128)(2,1)}, bf16[128,2048]{1,0:T(8,128)(2,1)}, f32[8,128]{1,0:T(8,128)}, f32[3,128,256]{2,1,0:T(8,128)}, f32[128,1024]{1,...) custom-call(bf16[128,2048]{1,0:T(8,128)(2,1)} %x_ref.1, ...), custom_call_target="tpu_custom_call" | custom-call | tf_op jit(solution)/shard_map/block_all/pallas_call | solution.py:828
  170.8 3.9 %give.1 = (bf16[128,2048]{1,0:T(8,128)(2,1)}, bf16[128,2048]{1,0:T(8,128)(2,1)}, f32[128]{0:T(128)}, f32[128]{0:T(128)}, f32[3,128,256]{2,1,0:T(8,128)}, /*index...) custom-call(bf16[128,2048]{1,0:T(8,128)(2,1)} %get-tuple-element.32., ...), custom_call_target="tpu_custom_call" | custom-call | tf_op jit(solution)/shard_map/give/pallas_call | solution.py:904
